TPU v7x, 32 devices: a whole 2x2x4 slice. The times are simulated.
32 devices in a mesh: dp: 8 (over z, y), section: 4 (over x, core).
Axes of the slice: x: 2, y: 2, z: 4, core: 2. Of those that a mesh axis runs over, the one named last changes fastest.
Arguments:
- frames: bfloat16 [32, 168, 512], P('dp'), may hold values from -6 to 6
- actions: int32 [32, 168], P('dp'), may hold values from 0 to 16
- deltas: int32 [32, 168, 4], P('dp'), may hold values from 0 to 1023
- kinds: int32 [32], P('dp'), may hold values from 0 to 1
- codebook: bfloat16 [1024, 512], replicated, may hold values from -3 to 3
- action_table: bfloat16 [17, 512], replicated, may hold values from -3 to 3
- position_table: bfloat16 [126, 512], replicated, may hold values from -3 to 3
- norm1_gain: float32 [2, 512], replicated, may hold values from 0.5 to 1.5
- norm1_bias: float32 [2, 512], replicated, may hold values from -1.25 to 1.25
- qkv_weight: bfloat16 [2, 512, 1536], replicated, may hold values from -0.25 to 0.25
- query_bias: float32 [2, 512], replicated, may hold values from -1.25 to 1.25
- value_bias: float32 [2, 512], replicated, may hold values from -1.25 to 1.25
- out_weight: bfloat16 [2, 512, 512], replicated, may hold values from -1 to 1
- out_bias: float32 [2, 512], replicated, may hold values from -1.25 to 1.25
- norm2_gain: float32 [2, 512], replicated, may hold values from 0.5 to 1.5
- norm2_bias: float32 [2, 512], replicated, may hold values from -1.25 to 1.25
- up_weight: bfloat16 [2, 512, 2048], replicated, may hold values from -0.25 to 0.25
- up_bias: float32 [2, 2048], replicated, may hold values from -1.25 to 1.25
- down_weight: bfloat16 [2, 2048, 512], replicated, may hold values from -0.125 to 0.125
- down_bias: float32 [2, 512], replicated, may hold values from -1.25 to 1.25
- final_gain: float32 [512], replicated, may hold values from 0.5 to 1.5
- final_bias: float32 [512], replicated, may hold values from -1.25 to 1.25
- cotangent: bfloat16 [32, 1008, 512], P('dp'), may hold values from -8 to 8
Outputs:
- activations: float32 [32, 1008, 512], P(('dp', 'section'))
- frame_grad: float32 [32, 168, 512], P(('dp', 'section'))
- codebook_grad: float32 [1024, 512], P(None, 'dp')
- action_grad: float32 [17, 512], P(None, 'dp')
- position_grad: float32 [126, 512], P(None, 'dp')
- norm1_gain_grad: float32 [2, 512], P(None, 'dp')
- norm1_bias_grad: float32 [2, 512], P(None, 'dp')
- qkv_grad: float32 [2, 512, 1536], P(None, 'dp')
- query_bias_grad: float32 [2, 512], P(None, 'dp')
- value_bias_grad: float32 [2, 512], P(None, 'dp')
- out_weight_grad: float32 [2, 512, 512], P(None, 'dp')
- out_bias_grad: float32 [2, 512], P(None, 'dp')
- norm2_gain_grad: float32 [2, 512], P(None, 'dp')
- norm2_bias_grad: float32 [2, 512], P(None, 'dp')
- up_weight_grad: float32 [2, 512, 2048], P(None, 'dp')
- up_bias_grad: float32 [2, 2048], P(None, 'dp')
- down_weight_grad: float32 [2, 2048, 512], P(None, None, 'dp')
- down_bias_grad: float32 [2, 512], P(None, 'dp')
- final_gain_grad: float32 [512], P('dp')
- final_bias_grad: float32 [512], P('dp')
Inputs may be any that keep to these rules, and one draw needn't show every extreme that they name: `kinds`: 1 marks a buffer of 8 sequences of 21 steps, 0 one of 21 sequences of 8 steps.
All inputs are finite; a program needn't handle non-finite values.
Results may differ from a plain program's by a relative error of at most 0.019.
Values may be sent and summed in bfloat16 or wider, within the bound.
No kernel may reach another device: no remote copies, remote signals or barrier semaphores. Data moves between devices by JAX's collectives and lax.ppermute only.
A program may use at most 448 MiB of HBM per device.

v0:
```python
from functools import partial

import jax
import jax.numpy as jnp
from jax import lax
from jax.sharding import PartitionSpec as P

HEADS = 8
SHORT_STEPS = 8
LONG_STEPS = 21


EPSILON = 1e-05
MASKED = -1e30
GRAD_DIMS = (1, 1, 1, 1, 1, 1, 1, 1, 1, 1, 1, 1, 1, 1, 2, 1, 0, 0)


def for_sending(array):
    return jax.tree.map(lambda a: a.astype(jnp.bfloat16) if a.dtype == jnp.float32 else a, array)


def passed_along(array, axis, by):
    size = lax.axis_size(axis)
    pairs = [(i, i + by) for i in range(size) if 0 <= i + by < size]
    return lax.ppermute(array, axis, pairs)


def norm_apply(hidden, gain, bias):
    center = hidden - jnp.mean(hidden, axis=-1, keepdims=True)
    spread = jnp.mean(center * center, axis=-1, keepdims=True)
    return center * lax.rsqrt(spread + EPSILON) * gain + bias


def plain_product(left, right):
    return jnp.dot(left, right, preferred_element_type=jnp.float32)


def left_product(left, right):
    return lax.dot_general(
        left, right, (((0,), (0,)), ((), ())), preferred_element_type=jnp.float32
    )


def right_product(left, right):
    return lax.dot_general(
        left, right, (((1,), (1,)), ((), ())), preferred_element_type=jnp.float32
    )


def token_layout(kind_value, steps, slots):
    span = jnp.where(kind_value == 1, LONG_STEPS, SHORT_STEPS).astype(jnp.int32)
    step_index = jnp.arange(steps, dtype=jnp.int32)
    slot_index = jnp.arange(slots, dtype=jnp.int32)
    position = ((step_index % span)[:, None] * slots + slot_index[None, :]).reshape(-1)
    token_step = jnp.repeat(step_index, slots)
    member = token_step // span
    allowed = (member[:, None] == member[None, :]) & (token_step[None, :] <= token_step[:, None])
    return (position, allowed)


def lookup_tables(tables, action_ids, delta_ids, position):
    codebook, action_table, position_table = tables
    action_hot = (
        action_ids[:, None] == jnp.arange(action_table.shape[0], dtype=jnp.int32)[None, :]
    ).astype(jnp.bfloat16)
    delta_hot = (
        delta_ids.reshape(-1)[:, None] == jnp.arange(codebook.shape[0], dtype=jnp.int32)[None, :]
    ).astype(jnp.bfloat16)
    place_hot = (
        position[:, None] == jnp.arange(position_table.shape[0], dtype=jnp.int32)[None, :]
    ).astype(jnp.bfloat16)
    return (action_hot, delta_hot, place_hot)


def embed_forward(tables, frame_rows, action_ids, delta_ids, position):
    codebook, action_table, position_table = tables
    action_hot, delta_hot, place_hot = lookup_tables(tables, action_ids, delta_ids, position)
    steps, width = frame_rows.shape
    action_rows = plain_product(action_hot, action_table)
    delta_rows = plain_product(delta_hot, codebook).reshape(steps, -1, width)
    tokens = jnp.concatenate(
        [frame_rows.astype(jnp.float32)[:, None], action_rows[:, None], delta_rows], axis=1
    ).reshape(-1, width)
    return (tokens + plain_product(place_hot, position_table)).astype(jnp.bfloat16)


def embed_backward(tables, action_ids, delta_ids, position, grad_bits):
    action_hot, delta_hot, place_hot = lookup_tables(tables, action_ids, delta_ids, position)
    rows, width = grad_bits.shape
    steps = action_ids.shape[0]
    per_slot = grad_bits.reshape(steps, rows // steps, width)
    frame_grad = per_slot[:, 0].astype(jnp.float32)
    grad_actions = left_product(action_hot, per_slot[:, 1])
    grad_codes = left_product(delta_hot, per_slot[:, 2:].reshape(-1, width))
    grad_places = left_product(place_hot, grad_bits)
    return (frame_grad, (grad_codes, grad_actions, grad_places))


def split_heads(qkv_bits, heads):
    rows = qkv_bits.shape[0]
    width = qkv_bits.shape[1] // 3
    head_dim = width // heads
    queries = qkv_bits[:, :width].reshape(rows, heads, head_dim)
    key_part = qkv_bits[:, width : 2 * width].reshape(rows, heads, head_dim)
    value_part = qkv_bits[:, 2 * width :].reshape(rows, heads, head_dim)
    return (queries, key_part, value_part)


def attention_probs(queries, key_part, allowed):
    scale = queries.shape[2] ** (-0.5)
    scores = (
        jnp.einsum("qhd,khd->hqk", queries, key_part, preferred_element_type=jnp.float32) * scale
    )
    scores = jnp.where(allowed[None], scores, MASKED)
    shifted = jnp.exp(scores - jnp.max(scores, axis=-1, keepdims=True))
    return shifted / jnp.sum(shifted, axis=-1, keepdims=True)


def layer_forward(hidden_bits, weights, allowed):
    (
        gain_first,
        bias_first,
        qkv_matrix,
        query_shift,
        value_shift,
        out_matrix,
        out_shift,
        gain_second,
        bias_second,
        up_matrix,
        up_shift,
        down_matrix,
        down_shift,
    ) = weights
    rows, width = hidden_bits.shape
    hidden = hidden_bits.astype(jnp.float32)
    normed = norm_apply(hidden, gain_first, bias_first).astype(jnp.bfloat16)
    shift = jnp.concatenate([query_shift, jnp.zeros_like(query_shift), value_shift])
    qkv_bits = (plain_product(normed, qkv_matrix) + shift).astype(jnp.bfloat16)
    queries, key_part, value_part = split_heads(qkv_bits, HEADS)
    probs = attention_probs(queries, key_part, allowed)
    mixed = jnp.einsum(
        "hqk,khd->qhd", probs.astype(jnp.bfloat16), value_part, preferred_element_type=jnp.float32
    )
    mixed_bits = mixed.reshape(rows, width).astype(jnp.bfloat16)
    middle = hidden + (plain_product(mixed_bits, out_matrix) + out_shift)
    normed_two = norm_apply(middle, gain_second, bias_second).astype(jnp.bfloat16)
    pre_act = plain_product(normed_two, up_matrix) + up_shift
    act_bits = jax.nn.gelu(pre_act, approximate=False).astype(jnp.bfloat16)
    output = middle + (plain_product(act_bits, down_matrix) + down_shift)
    return (output.astype(jnp.bfloat16), (hidden_bits, qkv_bits, mixed_bits, middle, pre_act))


def layer_backward(cache, weights, allowed, grad_bits):
    hidden_bits, qkv_bits, mixed_bits, middle, pre_act = cache
    (
        gain_first,
        bias_first,
        qkv_matrix,
        query_shift,
        value_shift,
        out_matrix,
        out_shift,
        gain_second,
        bias_second,
        up_matrix,
        up_shift,
        down_matrix,
        down_shift,
    ) = weights
    rows, width = hidden_bits.shape
    hidden = hidden_bits.astype(jnp.float32)
    act_value, gelu_pull = jax.vjp(partial(jax.nn.gelu, approximate=False), pre_act)
    act_bits = act_value.astype(jnp.bfloat16)
    normed_two = norm_apply(middle, gain_second, bias_second).astype(jnp.bfloat16)
    grad_down = left_product(act_bits, grad_bits)
    grad_down_shift = jnp.sum(grad_bits, axis=0, dtype=jnp.float32)
    grad_act = right_product(grad_bits, down_matrix)
    grad_pre_bits = gelu_pull(grad_act)[0].astype(jnp.bfloat16)
    grad_up = left_product(normed_two, grad_pre_bits)
    grad_up_shift = jnp.sum(grad_pre_bits, axis=0, dtype=jnp.float32)
    grad_normed_two = right_product(grad_pre_bits, up_matrix)
    second_pull = jax.vjp(norm_apply, middle, gain_second, bias_second)[1]
    grad_from_two, grad_gain_second, grad_bias_second = second_pull(grad_normed_two)
    grad_middle = grad_bits.astype(jnp.float32) + grad_from_two
    grad_middle_bits = grad_middle.astype(jnp.bfloat16)
    grad_out = left_product(mixed_bits, grad_middle_bits)
    grad_out_shift = jnp.sum(grad_middle_bits, axis=0, dtype=jnp.float32)
    queries, key_part, value_part = split_heads(qkv_bits, HEADS)
    scale = queries.shape[2] ** (-0.5)
    grad_mixed_bits = (
        right_product(grad_middle_bits, out_matrix).astype(jnp.bfloat16).reshape(queries.shape)
    )
    probs = attention_probs(queries, key_part, allowed)
    grad_probs = jnp.einsum(
        "qhd,khd->hqk", grad_mixed_bits, value_part, preferred_element_type=jnp.float32
    )
    grad_values = jnp.einsum(
        "hqk,qhd->khd",
        probs.astype(jnp.bfloat16),
        grad_mixed_bits,
        preferred_element_type=jnp.float32,
    )
    inner = jnp.sum(grad_probs * probs, axis=-1, keepdims=True)
    grad_scores = (probs * (grad_probs - inner)).astype(jnp.bfloat16)
    grad_queries = (
        jnp.einsum("hqk,khd->qhd", grad_scores, key_part, preferred_element_type=jnp.float32)
        * scale
    )
    grad_keys = (
        jnp.einsum("hqk,qhd->khd", grad_scores, queries, preferred_element_type=jnp.float32) * scale
    )
    grad_qkv_bits = jnp.concatenate(
        [
            grad_queries.reshape(rows, width),
            grad_keys.reshape(rows, width),
            grad_values.reshape(rows, width),
        ],
        axis=1,
    ).astype(jnp.bfloat16)
    normed = norm_apply(hidden, gain_first, bias_first).astype(jnp.bfloat16)
    grad_qkv = left_product(normed, grad_qkv_bits)
    grad_columns = jnp.sum(grad_qkv_bits, axis=0, dtype=jnp.float32)
    grad_normed = right_product(grad_qkv_bits, qkv_matrix)
    first_pull = jax.vjp(norm_apply, hidden, gain_first, bias_first)[1]
    grad_from_one, grad_gain_first, grad_bias_first = first_pull(grad_normed)
    grad_input = (grad_middle + grad_from_one).astype(jnp.bfloat16)
    terms = (
        grad_gain_first,
        grad_bias_first,
        grad_qkv,
        grad_columns[:width],
        grad_columns[2 * width :],
        grad_out,
        grad_out_shift,
        grad_gain_second,
        grad_bias_second,
        grad_up,
        grad_up_shift,
        grad_down,
        grad_down_shift,
    )
    return (grad_input, terms)


def add_terms(totals, terms, first):
    moved = tuple((total + term for total, term in zip(totals[first : first + len(terms)], terms)))
    return totals[:first] + moved + totals[first + len(terms) :]


def add_layer(totals, terms, depth):
    moved = tuple((total.at[depth].add(term) for total, term in zip(totals[3:16], terms)))
    return totals[:3] + moved + totals[16:]


def owner_rows(total, dim, parts):
    shape = total.shape
    split = shape[:dim] + (parts, shape[dim] // parts) + shape[dim + 1 :]
    return jnp.moveaxis(total.reshape(split), dim, 0).reshape(parts, -1)


def owner_shard(flat, total, dim, parts):
    shape = total.shape
    return flat.reshape(shape[:dim] + (shape[dim] // parts,) + shape[dim + 1 :])


def pack_totals(totals, groups):
    return jnp.concatenate(
        [owner_rows(total, dim, groups) for total, dim in zip(totals, GRAD_DIMS)], axis=1
    )


def unpack_totals(joined, totals, groups):
    pieces = []
    offset = 0
    for total, dim in zip(totals, GRAD_DIMS):
        count = total.size // groups
        pieces.append(owner_shard(joined[offset : offset + count], total, dim, groups))
        offset = offset + count
    return tuple(pieces)


def local(
    frames,
    actions,
    deltas,
    kinds,
    codebook,
    action_table,
    position_table,
    norm1_gain,
    norm1_bias,
    qkv_weight,
    query_bias,
    value_bias,
    out_weight,
    out_bias,
    norm2_gain,
    norm2_bias,
    up_weight,
    up_bias,
    down_weight,
    down_bias,
    final_gain,
    final_bias,
    cotangent,
):
    micro, steps, width = frames.shape
    rows = cotangent.shape[1]
    hidden_units = up_weight.shape[2]
    slots = rows // steps
    sections = lax.axis_size("section")
    section = lax.axis_index("section")
    tables = (codebook, action_table, position_table)
    layer_stack = (
        norm1_gain,
        norm1_bias,
        qkv_weight,
        query_bias,
        value_bias,
        out_weight,
        out_bias,
        norm2_gain,
        norm2_bias,
        up_weight,
        up_bias,
        down_weight,
        down_bias,
    )
    zero_totals = tuple(
        (
            jnp.zeros(weight.shape, jnp.float32)
            for weight in tables + layer_stack + (final_gain, final_bias)
        )
    )

    def layer_weights(depth):
        return tuple((weight[depth] for weight in layer_stack))

    def layout(slot):
        return token_layout(kinds[slot], steps, slots)

    def start_rows(slot):
        position = layout(slot)[0]
        return embed_forward(tables, frames[slot], actions[slot], deltas[slot], position)

    def finish_rows(slot, grad_bits):
        position = layout(slot)[0]
        return embed_backward(tables, actions[slot], deltas[slot], position, grad_bits)

    def final_rows(hidden_bits, grad_bits):
        output, pull = jax.vjp(norm_apply, hidden_bits.astype(jnp.float32), final_gain, final_bias)
        grad_hidden, grad_gain, grad_bias = pull(grad_bits.astype(jnp.float32))
        return (output, grad_hidden.astype(jnp.bfloat16), (grad_gain, grad_bias))

    zero_bits = jnp.zeros((rows, width), jnp.bfloat16)
    zero_rows = jnp.zeros((rows, width), jnp.float32)
    zero_frames = jnp.zeros((steps, width), jnp.float32)
    empty_cache = (
        zero_bits,
        jnp.zeros((rows, 3 * width), jnp.bfloat16),
        zero_bits,
        zero_rows,
        jnp.zeros((rows, hidden_units), jnp.float32),
    )
    kept_start = tuple((jnp.zeros((micro,) + piece.shape, piece.dtype) for piece in empty_cache))
    ticks = micro + sections - 1

    def forward_tick(tick, carry):
        arrived, kept, finals = carry
        slot_raw = tick - section
        valid = (slot_raw >= 0) & (slot_raw < micro)
        slot = jnp.clip(slot_raw, 0, micro - 1)
        allowed = layout(slot)[1]

        def forward_first_section():
            return (start_rows(slot), (arrived,) + empty_cache[1:], zero_rows)

        def layer_section(depth):

            def run_layer():
                sent, cache = layer_forward(arrived, layer_weights(depth), allowed)
                return (sent, cache, zero_rows)

            return run_layer

        def forward_last_section():
            output = norm_apply(arrived.astype(jnp.float32), final_gain, final_bias)
            return (zero_bits, (arrived,) + empty_cache[1:], output)

        sent, cache, output = lax.switch(
            section,
            [forward_first_section, layer_section(0), layer_section(1), forward_last_section],
        )
        kept = tuple(
            (
                lax.dynamic_update_index_in_dim(
                    store, jnp.where(valid, piece, store[slot]), slot, 0
                )
                for store, piece in zip(kept, cache)
            )
        )
        finals = lax.dynamic_update_index_in_dim(
            finals, jnp.where(valid, output, finals[slot]), slot, 0
        )
        arrived = jax.tree.map(
            lambda part, own: part.astype(own.dtype),
            passed_along(for_sending(sent), "section", 1),
            sent,
        )
        return (arrived, kept, finals)

    unused, kept, finals = lax.fori_loop(
        0,
        ticks,
        forward_tick,
        (zero_bits, kept_start, jnp.zeros((micro, rows, width), jnp.float32)),
    )

    def backward_tick(tick, carry):
        arrived, totals, frame_store = carry
        slot_raw = tick - (sections - 1 - section)
        valid = (slot_raw >= 0) & (slot_raw < micro)
        slot = jnp.clip(slot_raw, 0, micro - 1)
        allowed = layout(slot)[1]
        cache = tuple((store[slot] for store in kept))

        def backward_first_section():
            frame_grad, terms = finish_rows(slot, arrived)
            return (zero_bits, add_terms(totals, terms, 0), frame_grad)

        def layer_section(depth):

            def run_layer():
                sent, terms = layer_backward(cache, layer_weights(depth), allowed, arrived)
                return (sent, add_layer(totals, terms, depth), zero_frames)

            return run_layer

        def backward_last_section():
            grad_bits = jnp.where(valid, cotangent[slot], jnp.zeros_like(cotangent[slot]))
            output, sent, terms = final_rows(cache[0], grad_bits)
            return (sent, add_terms(totals, terms, 16), zero_frames)

        sent, totals, frame_grad = lax.switch(
            section,
            [backward_first_section, layer_section(0), layer_section(1), backward_last_section],
        )
        frame_store = lax.dynamic_update_index_in_dim(
            frame_store, jnp.where(valid, frame_grad, frame_store[slot]), slot, 0
        )
        arrived = jax.tree.map(
            lambda part, own: part.astype(own.dtype),
            passed_along(for_sending(sent), "section", -1),
            sent,
        )
        return (arrived, totals, frame_store)

    unused, totals, frame_store = lax.fori_loop(
        0,
        ticks,
        backward_tick,
        (zero_bits, zero_totals, jnp.zeros((micro, steps, width), jnp.float32)),
    )
    joined_out = jnp.concatenate([finals, frame_store], axis=1)
    outputs_shard = lax.psum_scatter(
        joined_out.astype(jnp.bfloat16), "section", scatter_dimension=0, tiled=True
    ).astype(jnp.float32)
    finals_shard = outputs_shard[:, :rows]
    frames_shard = outputs_shard[:, rows:]
    groups = lax.axis_size("dp")
    packed = pack_totals(totals, groups)
    wide = lax.psum_scatter(packed, "dp", scatter_dimension=0, tiled=True)
    summed_row = lax.psum(wide.astype(jnp.bfloat16), "section").astype(jnp.float32)[0]
    summed = unpack_totals(summed_row, totals, groups)
    return (finals_shard, frames_shard) + tuple(summed)


def solution(mesh):
    return jax.shard_map(
        local,
        mesh=mesh,
        in_specs=(
            P("dp", None, None),
            P("dp", None),
            P("dp", None, None),
            P("dp"),
            P(),
            P(),
            P(),
            P(),
            P(),
            P(),
            P(),
            P(),
            P(),
            P(),
            P(),
            P(),
            P(),
            P(),
            P(),
            P(),
            P(),
            P(),
            P("dp", None, None),
        ),
        out_specs=(
            P(("dp", "section"), None, None),
            P(("dp", "section"), None, None),
            P(None, "dp"),
            P(None, "dp"),
            P(None, "dp"),
            P(None, "dp"),
            P(None, "dp"),
            P(None, "dp", None),
            P(None, "dp"),
            P(None, "dp"),
            P(None, "dp", None),
            P(None, "dp"),
            P(None, "dp"),
            P(None, "dp"),
            P(None, "dp", None),
            P(None, "dp"),
            P(None, None, "dp"),
            P(None, "dp"),
            P("dp"),
            P("dp"),
        ),
        check_vma=False,
    )
```

profile of v0, /device:TPU:0, one launch (start us, length us, event | category | flops | bytes accessed | tf_op | source)
XLA Modules:
  0.0 4246.0 jit_solution(6617112850964591131)
XLA Ops:
  37.0 1074.7 %while.106 = (s32[]{:T(128)}, bf16[1008,512]{1,0:T(8,128)(2,1)S(1)}, bf16[4,1008,512]{2,1,0:T(8,128)(2,1)}, bf16[4,1008,1536]{2,1,0:T(8,128)(2,1)}, bf16[4,1008,...) while((s32[]{:T(128)}, bf16[1008,512]{1,0:T(8,128)(2,1)S(1)}, ...), condition=%wide.region_19.20_spmd, body=%wide.region_0.19_spmd.sunk | while | flops 8634001408 | bytes 275782240 | solution.py:413
  37.3 41.8 conditional.4
  79.2 65.7 %collective-permute-start = (bf16[1008,512]{1,0:T(8,128)(2,1)}, bf16[1008,512]{1,0:T(8,128)(2,1)}, u32[]{:S(2)}, u32[]{:S(2)}) collective-permute-start(bf16[1008,512]{1,0:T(8,128)(2,1)} %get-tuple-element.5125), channel_id=1, source_target_pairs={{0,1},{1,2},{2,3},{4,5},{5,6},{6,7},{8,9},{9,10},{10,11},{12,13},{... | collective-permute-start | bytes 3096584 | tf_op jit(solution)/shard_map/while/body/eval_jaxpr/ppermute | solution.py:25
  192.5 41.8 conditional.4
  234.3 62.9 %collective-permute-start = (bf16[1008,512]{1,0:T(8,128)(2,1)}, bf16[1008,512]{1,0:T(8,128)(2,1)}, u32[]{:S(2)}, u32[]{:S(2)}) collective-permute-start(bf16[1008,512]{1,0:T(8,128)(2,1)} %get-tuple-element.5125), channel_id=1, source_target_pairs={{0,1},{1,2},{2,3},{4,5},{5,6},{6,7},{8,9},{9,10},{10,11},{12,13},{... | collective-permute-start | bytes 3096584 | tf_op jit(solution)/shard_map/while/body/eval_jaxpr/ppermute | solution.py:25
  386.3 68.7 %collective-permute-start = (bf16[1008,512]{1,0:T(8,128)(2,1)}, bf16[1008,512]{1,0:T(8,128)(2,1)}, u32[]{:S(2)}, u32[]{:S(2)}) collective-permute-start(bf16[1008,512]{1,0:T(8,128)(2,1)} %get-tuple-element.5125), channel_id=1, source_target_pairs={{0,1},{1,2},{2,3},{4,5},{5,6},{6,7},{8,9},{9,10},{10,11},{12,13},{... | collective-permute-start | bytes 3096584 | tf_op jit(solution)/shard_map/while/body/eval_jaxpr/ppermute | solution.py:25
  502.4 41.8 conditional.4
  544.2 64.0 %collective-permute-start = (bf16[1008,512]{1,0:T(8,128)(2,1)}, bf16[1008,512]{1,0:T(8,128)(2,1)}, u32[]{:S(2)}, u32[]{:S(2)}) collective-permute-start(bf16[1008,512]{1,0:T(8,128)(2,1)} %get-tuple-element.5125), channel_id=1, source_target_pairs={{0,1},{1,2},{2,3},{4,5},{5,6},{6,7},{8,9},{9,10},{10,11},{12,13},{... | collective-permute-start | bytes 3096584 | tf_op jit(solution)/shard_map/while/body/eval_jaxpr/ppermute | solution.py:25
  655.7 41.7 conditional.4
  697.4 64.8 %collective-permute-start = (bf16[1008,512]{1,0:T(8,128)(2,1)}, bf16[1008,512]{1,0:T(8,128)(2,1)}, u32[]{:S(2)}, u32[]{:S(2)}) collective-permute-start(bf16[1008,512]{1,0:T(8,128)(2,1)} %get-tuple-element.5125), channel_id=1, source_target_pairs={{0,1},{1,2},{2,3},{4,5},{5,6},{6,7},{8,9},{9,10},{10,11},{12,13},{... | collective-permute-start | bytes 3096584 | tf_op jit(solution)/shard_map/while/body/eval_jaxpr/ppermute | solution.py:25
  802.1 41.8 conditional.4
  843.9 75.8 %collective-permute-start = (bf16[1008,512]{1,0:T(8,128)(2,1)}, bf16[1008,512]{1,0:T(8,128)(2,1)}, u32[]{:S(2)}, u32[]{:S(2)}) collective-permute-start(bf16[1008,512]{1,0:T(8,128)(2,1)} %get-tuple-element.5125), channel_id=1, source_target_pairs={{0,1},{1,2},{2,3},{4,5},{5,6},{6,7},{8,9},{9,10},{10,11},{12,13},{... | collective-permute-start | bytes 3096584 | tf_op jit(solution)/shard_map/while/body/eval_jaxpr/ppermute | solution.py:25
  959.4 41.7 conditional.4
  1001.2 68.4 %collective-permute-start = (bf16[1008,512]{1,0:T(8,128)(2,1)}, bf16[1008,512]{1,0:T(8,128)(2,1)}, u32[]{:S(2)}, u32[]{:S(2)}) collective-permute-start(bf16[1008,512]{1,0:T(8,128)(2,1)} %get-tuple-element.5125), channel_id=1, source_target_pairs={{0,1},{1,2},{2,3},{4,5},{5,6},{6,7},{8,9},{9,10},{10,11},{12,13},{... | collective-permute-start | bytes 3096584 | tf_op jit(solution)/shard_map/while/body/eval_jaxpr/ppermute | solution.py:25
  1150.7 1724.0 %while.107 = (s32[]{:T(128)}, bf16[1008,512]{1,0:T(8,128)(2,1)S(1)}, f32[1024,512]{1,0:T(8,128)}, f32[17,512]{1,0:T(8,128)}, f32[126,512]{1,0:T(8,128)}, /*index...) while((s32[]{:T(128)}, bf16[1008,512]{1,0:T(8,128)(2,1)S(1)}, ...), condition=%wide.region_69.70_spmd, body=%wide.region_20.69_spmd.sunk | while | flops 18234163200 | bytes 544712960 | solution.py:459
  1186.1 208.5 %collective-permute-done.1 = bf16[1008,512]{1,0:T(8,128)(2,1)S(1)} collective-permute-done((bf16[1008,512]{1,0:T(8,128)(2,1)}, bf16[1008,512]{1,0:T(8,128)(2,1)S(1)}, u32[]{:S(2)}, u32[]{:S(2)}) %collective-permute-start.1) | collective-permute-done | bytes 1032224 | tf_op jit(solution)/shard_map/while/body/eval_jaxpr/ppermute | solution.py:25
  1413.0 226.8 %collective-permute-done.1 = bf16[1008,512]{1,0:T(8,128)(2,1)S(1)} collective-permute-done((bf16[1008,512]{1,0:T(8,128)(2,1)}, bf16[1008,512]{1,0:T(8,128)(2,1)S(1)}, u32[]{:S(2)}, u32[]{:S(2)}) %collective-permute-start.1) | collective-permute-done | bytes 1032224 | tf_op jit(solution)/shard_map/while/body/eval_jaxpr/ppermute | solution.py:25
  1657.8 227.0 %collective-permute-done.1 = bf16[1008,512]{1,0:T(8,128)(2,1)S(1)} collective-permute-done((bf16[1008,512]{1,0:T(8,128)(2,1)}, bf16[1008,512]{1,0:T(8,128)(2,1)S(1)}, u32[]{:S(2)}, u32[]{:S(2)}) %collective-permute-start.1) | collective-permute-done | bytes 1032224 | tf_op jit(solution)/shard_map/while/body/eval_jaxpr/ppermute | solution.py:25
  1902.9 227.0 %collective-permute-done.1 = bf16[1008,512]{1,0:T(8,128)(2,1)S(1)} collective-permute-done((bf16[1008,512]{1,0:T(8,128)(2,1)}, bf16[1008,512]{1,0:T(8,128)(2,1)S(1)}, u32[]{:S(2)}, u32[]{:S(2)}) %collective-permute-start.1) | collective-permute-done | bytes 1032224 | tf_op jit(solution)/shard_map/while/body/eval_jaxpr/ppermute | solution.py:25
  2148.0 227.0 %collective-permute-done.1 = bf16[1008,512]{1,0:T(8,128)(2,1)S(1)} collective-permute-done((bf16[1008,512]{1,0:T(8,128)(2,1)}, bf16[1008,512]{1,0:T(8,128)(2,1)S(1)}, u32[]{:S(2)}, u32[]{:S(2)}) %collective-permute-start.1) | collective-permute-done | bytes 1032224 | tf_op jit(solution)/shard_map/while/body/eval_jaxpr/ppermute | solution.py:25
  2393.2 227.0 %collective-permute-done.1 = bf16[1008,512]{1,0:T(8,128)(2,1)S(1)} collective-permute-done((bf16[1008,512]{1,0:T(8,128)(2,1)}, bf16[1008,512]{1,0:T(8,128)(2,1)S(1)}, u32[]{:S(2)}, u32[]{:S(2)}) %collective-permute-start.1) | collective-permute-done | bytes 1032224 | tf_op jit(solution)/shard_map/while/body/eval_jaxpr/ppermute | solution.py:25
  2638.3 227.0 %collective-permute-done.1 = bf16[1008,512]{1,0:T(8,128)(2,1)S(1)} collective-permute-done((bf16[1008,512]{1,0:T(8,128)(2,1)}, bf16[1008,512]{1,0:T(8,128)(2,1)S(1)}, u32[]{:S(2)}, u32[]{:S(2)}) %collective-permute-start.1) | collective-permute-done | bytes 1032224 | tf_op jit(solution)/shard_map/while/body/eval_jaxpr/ppermute | solution.py:25
  3041.3 1057.7 %all-reduce.5 = bf16[8,862784]{1,0:T(8,128)(2,1)} all-reduce(f32[8,862784]{1,0:T(8,128)} %constant_dynamic-update-slice_fusion), channel_id=3, replica_groups=mesh['dp'=8,'section'=4] {'dp'}, use_global_device_ids=true, to_apply=%region_71.72.clone | all-reduce | flops 6902272 | bytes 41413632
  4113.2 67.0 %all-reduce.4.cloned.1.call-done = bf16[1,862784]{1,0:T(2,128)(2,1)} async-done(((bf16[1,862784]{1,0:T(2,128)(2,1)}), bf16[1,862784]{1,0:T(2,128)(2,1)}) %all-reduce.4.cloned.1.call-update) | async-done | bytes 1725584 | tf_op jit(solution)/shard_map/psum | solution.py:474
  (671 shorter events, 1064.5 us)
Async XLA Ops:
  7.2 4173.0 %all-reduce.4.cloned.1.call-start = ((), (), s32[]{:S(2)}) async-start(), calls=%async_computation.2 | async-start | bytes 6902784 | tf_op jit(solution)/shard_map/psum | solution.py:474
  79.2 111.7 %collective-permute-start = (bf16[1008,512]{1,0:T(8,128)(2,1)}, bf16[1008,512]{1,0:T(8,128)(2,1)}, u32[]{:S(2)}, u32[]{:S(2)}) collective-permute-start(bf16[1008,512]{1,0:T(8,128)(2,1)} %get-tuple-element.5125), channel_id=1, source_target_pairs={{0,1},{1,2},{2,3},{4,5},{5,6},{6,7},{8,9},{9,10},{10,11},{12,13},{... | collective-permute-start | bytes 3096584 | tf_op jit(solution)/shard_map/while/body/eval_jaxpr/ppermute | solution.py:25
  234.3 108.8 %collective-permute-start = (bf16[1008,512]{1,0:T(8,128)(2,1)}, bf16[1008,512]{1,0:T(8,128)(2,1)}, u32[]{:S(2)}, u32[]{:S(2)}) collective-permute-start(bf16[1008,512]{1,0:T(8,128)(2,1)} %get-tuple-element.5125), channel_id=1, source_target_pairs={{0,1},{1,2},{2,3},{4,5},{5,6},{6,7},{8,9},{9,10},{10,11},{12,13},{... | collective-permute-start | bytes 3096584 | tf_op jit(solution)/shard_map/while/body/eval_jaxpr/ppermute | solution.py:25
  331.5 12.9 copy-start.31
  386.3 114.5 %collective-permute-start = (bf16[1008,512]{1,0:T(8,128)(2,1)}, bf16[1008,512]{1,0:T(8,128)(2,1)}, u32[]{:S(2)}, u32[]{:S(2)}) collective-permute-start(bf16[1008,512]{1,0:T(8,128)(2,1)} %get-tuple-element.5125), channel_id=1, source_target_pairs={{0,1},{1,2},{2,3},{4,5},{5,6},{6,7},{8,9},{9,10},{10,11},{12,13},{... | collective-permute-start | bytes 3096584 | tf_op jit(solution)/shard_map/while/body/eval_jaxpr/ppermute | solution.py:25
  544.2 110.0 %collective-permute-start = (bf16[1008,512]{1,0:T(8,128)(2,1)}, bf16[1008,512]{1,0:T(8,128)(2,1)}, u32[]{:S(2)}, u32[]{:S(2)}) collective-permute-start(bf16[1008,512]{1,0:T(8,128)(2,1)} %get-tuple-element.5125), channel_id=1, source_target_pairs={{0,1},{1,2},{2,3},{4,5},{5,6},{6,7},{8,9},{9,10},{10,11},{12,13},{... | collective-permute-start | bytes 3096584 | tf_op jit(solution)/shard_map/while/body/eval_jaxpr/ppermute | solution.py:25
  642.5 12.9 copy-start.22
  642.6 12.9 copy-start.26
  642.6 12.9 copy-start.29
  642.6 12.9 copy-start.31
  697.4 103.0 %collective-permute-start = (bf16[1008,512]{1,0:T(8,128)(2,1)}, bf16[1008,512]{1,0:T(8,128)(2,1)}, u32[]{:S(2)}, u32[]{:S(2)}) collective-permute-start(bf16[1008,512]{1,0:T(8,128)(2,1)} %get-tuple-element.5125), channel_id=1, source_target_pairs={{0,1},{1,2},{2,3},{4,5},{5,6},{6,7},{8,9},{9,10},{10,11},{12,13},{... | collective-permute-start | bytes 3096584 | tf_op jit(solution)/shard_map/while/body/eval_jaxpr/ppermute | solution.py:25
  843.9 114.1 %collective-permute-start = (bf16[1008,512]{1,0:T(8,128)(2,1)}, bf16[1008,512]{1,0:T(8,128)(2,1)}, u32[]{:S(2)}, u32[]{:S(2)}) collective-permute-start(bf16[1008,512]{1,0:T(8,128)(2,1)} %get-tuple-element.5125), channel_id=1, source_target_pairs={{0,1},{1,2},{2,3},{4,5},{5,6},{6,7},{8,9},{9,10},{10,11},{12,13},{... | collective-permute-start | bytes 3096584 | tf_op jit(solution)/shard_map/while/body/eval_jaxpr/ppermute | solution.py:25
  1001.2 106.6 %collective-permute-start = (bf16[1008,512]{1,0:T(8,128)(2,1)}, bf16[1008,512]{1,0:T(8,128)(2,1)}, u32[]{:S(2)}, u32[]{:S(2)}) collective-permute-start(bf16[1008,512]{1,0:T(8,128)(2,1)} %get-tuple-element.5125), channel_id=1, source_target_pairs={{0,1},{1,2},{2,3},{4,5},{5,6},{6,7},{8,9},{9,10},{10,11},{12,13},{... | collective-permute-start | bytes 3096584 | tf_op jit(solution)/shard_map/while/body/eval_jaxpr/ppermute | solution.py:25
  1183.2 211.5 %collective-permute-start.1 = (bf16[1008,512]{1,0:T(8,128)(2,1)}, bf16[1008,512]{1,0:T(8,128)(2,1)S(1)}, u32[]{:S(2)}, u32[]{:S(2)}) collective-permute-start(bf16[1008,512]{1,0:T(8,128)(2,1)} %get-tuple-element.5174), channel_id=1, source_target_pairs={{1,0},{2,1},{3,2},{5,4},{6,5},{7,6},{9,8},{10,9},{11,10},{13,12},{... | collective-permute-start | bytes 3096584 | tf_op jit(solution)/shard_map/while/body/eval_jaxpr/ppermute | solution.py:25
  1410.0 229.7 %collective-permute-start.1 = (bf16[1008,512]{1,0:T(8,128)(2,1)}, bf16[1008,512]{1,0:T(8,128)(2,1)S(1)}, u32[]{:S(2)}, u32[]{:S(2)}) collective-permute-start(bf16[1008,512]{1,0:T(8,128)(2,1)} %get-tuple-element.5174), channel_id=1, source_target_pairs={{1,0},{2,1},{3,2},{5,4},{6,5},{7,6},{9,8},{10,9},{11,10},{13,12},{... | collective-permute-start | bytes 3096584 | tf_op jit(solution)/shard_map/while/body/eval_jaxpr/ppermute | solution.py:25
  1654.9 230.0 %collective-permute-start.1 = (bf16[1008,512]{1,0:T(8,128)(2,1)}, bf16[1008,512]{1,0:T(8,128)(2,1)S(1)}, u32[]{:S(2)}, u32[]{:S(2)}) collective-permute-start(bf16[1008,512]{1,0:T(8,128)(2,1)} %get-tuple-element.5174), channel_id=1, source_target_pairs={{1,0},{2,1},{3,2},{5,4},{6,5},{7,6},{9,8},{10,9},{11,10},{13,12},{... | collective-permute-start | bytes 3096584 | tf_op jit(solution)/shard_map/while/body/eval_jaxpr/ppermute | solution.py:25
  1900.0 230.0 %collective-permute-start.1 = (bf16[1008,512]{1,0:T(8,128)(2,1)}, bf16[1008,512]{1,0:T(8,128)(2,1)S(1)}, u32[]{:S(2)}, u32[]{:S(2)}) collective-permute-start(bf16[1008,512]{1,0:T(8,128)(2,1)} %get-tuple-element.5174), channel_id=1, source_target_pairs={{1,0},{2,1},{3,2},{5,4},{6,5},{7,6},{9,8},{10,9},{11,10},{13,12},{... | collective-permute-start | bytes 3096584 | tf_op jit(solution)/shard_map/while/body/eval_jaxpr/ppermute | solution.py:25
  2145.1 230.0 %collective-permute-start.1 = (bf16[1008,512]{1,0:T(8,128)(2,1)}, bf16[1008,512]{1,0:T(8,128)(2,1)S(1)}, u32[]{:S(2)}, u32[]{:S(2)}) collective-permute-start(bf16[1008,512]{1,0:T(8,128)(2,1)} %get-tuple-element.5174), channel_id=1, source_target_pairs={{1,0},{2,1},{3,2},{5,4},{6,5},{7,6},{9,8},{10,9},{11,10},{13,12},{... | collective-permute-start | bytes 3096584 | tf_op jit(solution)/shard_map/while/body/eval_jaxpr/ppermute | solution.py:25
  2390.2 230.0 %collective-permute-start.1 = (bf16[1008,512]{1,0:T(8,128)(2,1)}, bf16[1008,512]{1,0:T(8,128)(2,1)S(1)}, u32[]{:S(2)}, u32[]{:S(2)}) collective-permute-start(bf16[1008,512]{1,0:T(8,128)(2,1)} %get-tuple-element.5174), channel_id=1, source_target_pairs={{1,0},{2,1},{3,2},{5,4},{6,5},{7,6},{9,8},{10,9},{11,10},{13,12},{... | collective-permute-start | bytes 3096584 | tf_op jit(solution)/shard_map/while/body/eval_jaxpr/ppermute | solution.py:25
  2635.3 230.0 %collective-permute-start.1 = (bf16[1008,512]{1,0:T(8,128)(2,1)}, bf16[1008,512]{1,0:T(8,128)(2,1)S(1)}, u32[]{:S(2)}, u32[]{:S(2)}) collective-permute-start(bf16[1008,512]{1,0:T(8,128)(2,1)} %get-tuple-element.5174), channel_id=1, source_target_pairs={{1,0},{2,1},{3,2},{5,4},{6,5},{7,6},{9,8},{10,9},{11,10},{13,12},{... | collective-permute-start | bytes 3096584 | tf_op jit(solution)/shard_map/while/body/eval_jaxpr/ppermute | solution.py:25
  2892.2 13.5 slice-start.4
  2956.9 21.3 copy-start.23
  3041.3 1057.7 %copy-start.74 = (u32[32]{0:T(128)S(1)}, u32[32]{0:T(128)}, u32[]{:S(2)}) copy-start(u32[32]{0:T(128)} %constant.1814) | copy-start | bytes 388
  4108.4 126.1 %reduce-scatter.2.cloned.1.call-start = ((), (), s32[]{:S(2)}) async-start(), calls=%async_computation.1 | async-start | bytes 6021120 | tf_op jit(solution)/shard_map/reduce_scatter | solution.py:466
  (60 other events, 571.4 us)
Sparse Core Ops, SparseCore 0:
  4108.5 71.7 all-reduce.3
  4182.9 48.5 reduce-scatter.1
where the time goes:
time: 4260 us; the launch traced here: 4250 us
  waiting for transfers between devices  1640 us (38%)
  blocking collectives  1060 us (25%)
  local copies, waits for them, and re-layouts  610 us (14%)
  starting transfers between devices  479 us (11%)
  other arithmetic  199 us (5%)
  loops' own time  157 us (4%)
  matrix products  90.5 us (2%)
    ppermute x14, waiting for transfers between devices, passed_along(): return lax.ppermute(array, axis, pairs)  1570 us
    unnamed x1, blocking collectives  1060 us
    ppermute x14, starting transfers between devices, passed_along(): return lax.ppermute(array, axis, pairs)  479 us
    dynamic_update_slice x28, other arithmetic, forward_tick(): lax.dynamic_update_index_in_dim(store, jnp.where(valid, piece, store[slot...  137 us
    dynamic_slice x35, local copies, waits for them, and re-layouts, forward_tick(): store[slot]  124 us
    another operation x7, loops' own time, forward_tick(): lax.switch(section, [forward_first_section, layer_section(0), layer_secti...  119 us
    unnamed x60, local copies, waits for them, and re-layouts  99.1 us
  transfers between devices with their start and end apart: 16, of which 8 were waited for; matrix products, arithmetic and copies ran while one was open for 9% of the time, Pallas kernels for 0%

commit v1 on v0

--- a/solution.py
+++ b/solution.py
@@ -243,41 +243,9 @@
     return (grad_input, terms)
 
 
-def add_terms(totals, terms, first):
-    moved = tuple((total + term for total, term in zip(totals[first : first + len(terms)], terms)))
-    return totals[:first] + moved + totals[first + len(terms) :]
-
-
-def add_layer(totals, terms, depth):
-    moved = tuple((total.at[depth].add(term) for total, term in zip(totals[3:16], terms)))
-    return totals[:3] + moved + totals[16:]
-
-
-def owner_rows(total, dim, parts):
-    shape = total.shape
-    split = shape[:dim] + (parts, shape[dim] // parts) + shape[dim + 1 :]
-    return jnp.moveaxis(total.reshape(split), dim, 0).reshape(parts, -1)
-
-
-def owner_shard(flat, total, dim, parts):
-    shape = total.shape
-    return flat.reshape(shape[:dim] + (shape[dim] // parts,) + shape[dim + 1 :])
-
-
-def pack_totals(totals, groups):
-    return jnp.concatenate(
-        [owner_rows(total, dim, groups) for total, dim in zip(totals, GRAD_DIMS)], axis=1
-    )
-
-
-def unpack_totals(joined, totals, groups):
-    pieces = []
-    offset = 0
-    for total, dim in zip(totals, GRAD_DIMS):
-        count = total.size // groups
-        pieces.append(owner_shard(joined[offset : offset + count], total, dim, groups))
-        offset = offset + count
-    return tuple(pieces)
+def reduced(matrix):
+    shard = lax.psum_scatter(matrix.astype(jnp.bfloat16), ("dp", "section"), scatter_dimension=0, tiled=True)
+    return lax.all_gather(shard, "section", axis=0, tiled=True).astype(jnp.float32)
 
 
 def local(
@@ -307,10 +275,10 @@
 ):
     micro, steps, width = frames.shape
     rows = cotangent.shape[1]
-    hidden_units = up_weight.shape[2]
     slots = rows // steps
     sections = lax.axis_size("section")
     section = lax.axis_index("section")
+    per = micro // sections
     tables = (codebook, action_table, position_table)
     layer_stack = (
         norm1_gain,
@@ -327,153 +295,83 @@
         down_weight,
         down_bias,
     )
-    zero_totals = tuple(
-        (
-            jnp.zeros(weight.shape, jnp.float32)
-            for weight in tables + layer_stack + (final_gain, final_bias)
-        )
-    )
 
     def layer_weights(depth):
         return tuple((weight[depth] for weight in layer_stack))
 
-    def layout(slot):
-        return token_layout(kinds[slot], steps, slots)
-
-    def start_rows(slot):
-        position = layout(slot)[0]
-        return embed_forward(tables, frames[slot], actions[slot], deltas[slot], position)
-
-    def finish_rows(slot, grad_bits):
-        position = layout(slot)[0]
-        return embed_backward(tables, actions[slot], deltas[slot], position, grad_bits)
-
-    def final_rows(hidden_bits, grad_bits):
-        output, pull = jax.vjp(norm_apply, hidden_bits.astype(jnp.float32), final_gain, final_bias)
-        grad_hidden, grad_gain, grad_bias = pull(grad_bits.astype(jnp.float32))
-        return (output, grad_hidden.astype(jnp.bfloat16), (grad_gain, grad_bias))
-
-    zero_bits = jnp.zeros((rows, width), jnp.bfloat16)
-    zero_rows = jnp.zeros((rows, width), jnp.float32)
-    zero_frames = jnp.zeros((steps, width), jnp.float32)
-    empty_cache = (
-        zero_bits,
-        jnp.zeros((rows, 3 * width), jnp.bfloat16),
-        zero_bits,
-        zero_rows,
-        jnp.zeros((rows, hidden_units), jnp.float32),
-    )
-    kept_start = tuple((jnp.zeros((micro,) + piece.shape, piece.dtype) for piece in empty_cache))
-    ticks = micro + sections - 1
-
-    def forward_tick(tick, carry):
-        arrived, kept, finals = carry
-        slot_raw = tick - section
-        valid = (slot_raw >= 0) & (slot_raw < micro)
-        slot = jnp.clip(slot_raw, 0, micro - 1)
-        allowed = layout(slot)[1]
-
-        def forward_first_section():
-            return (start_rows(slot), (arrived,) + empty_cache[1:], zero_rows)
-
-        def layer_section(depth):
-
-            def run_layer():
-                sent, cache = layer_forward(arrived, layer_weights(depth), allowed)
-                return (sent, cache, zero_rows)
-
-            return run_layer
-
-        def forward_last_section():
-            output = norm_apply(arrived.astype(jnp.float32), final_gain, final_bias)
-            return (zero_bits, (arrived,) + empty_cache[1:], output)
-
-        sent, cache, output = lax.switch(
-            section,
-            [forward_first_section, layer_section(0), layer_section(1), forward_last_section],
-        )
-        kept = tuple(
-            (
-                lax.dynamic_update_index_in_dim(
-                    store, jnp.where(valid, piece, store[slot]), slot, 0
-                )
-                for store, piece in zip(kept, cache)
-            )
-        )
-        finals = lax.dynamic_update_index_in_dim(
-            finals, jnp.where(valid, output, finals[slot]), slot, 0
-        )
-        arrived = jax.tree.map(
-            lambda part, own: part.astype(own.dtype),
-            passed_along(for_sending(sent), "section", 1),
-            sent,
-        )
-        return (arrived, kept, finals)
-
-    unused, kept, finals = lax.fori_loop(
-        0,
-        ticks,
-        forward_tick,
-        (zero_bits, kept_start, jnp.zeros((micro, rows, width), jnp.float32)),
-    )
-
-    def backward_tick(tick, carry):
-        arrived, totals, frame_store = carry
-        slot_raw = tick - (sections - 1 - section)
-        valid = (slot_raw >= 0) & (slot_raw < micro)
-        slot = jnp.clip(slot_raw, 0, micro - 1)
-        allowed = layout(slot)[1]
-        cache = tuple((store[slot] for store in kept))
-
-        def backward_first_section():
-            frame_grad, terms = finish_rows(slot, arrived)
-            return (zero_bits, add_terms(totals, terms, 0), frame_grad)
-
-        def layer_section(depth):
-
-            def run_layer():
-                sent, terms = layer_backward(cache, layer_weights(depth), allowed, arrived)
-                return (sent, add_layer(totals, terms, depth), zero_frames)
-
-            return run_layer
-
-        def backward_last_section():
-            grad_bits = jnp.where(valid, cotangent[slot], jnp.zeros_like(cotangent[slot]))
-            output, sent, terms = final_rows(cache[0], grad_bits)
-            return (sent, add_terms(totals, terms, 16), zero_frames)
-
-        sent, totals, frame_grad = lax.switch(
-            section,
-            [backward_first_section, layer_section(0), layer_section(1), backward_last_section],
-        )
-        frame_store = lax.dynamic_update_index_in_dim(
-            frame_store, jnp.where(valid, frame_grad, frame_store[slot]), slot, 0
-        )
-        arrived = jax.tree.map(
-            lambda part, own: part.astype(own.dtype),
-            passed_along(for_sending(sent), "section", -1),
-            sent,
-        )
-        return (arrived, totals, frame_store)
-
-    unused, totals, frame_store = lax.fori_loop(
-        0,
-        ticks,
-        backward_tick,
-        (zero_bits, zero_totals, jnp.zeros((micro, steps, width), jnp.float32)),
-    )
-    joined_out = jnp.concatenate([finals, frame_store], axis=1)
-    outputs_shard = lax.psum_scatter(
-        joined_out.astype(jnp.bfloat16), "section", scatter_dimension=0, tiled=True
-    ).astype(jnp.float32)
-    finals_shard = outputs_shard[:, :rows]
-    frames_shard = outputs_shard[:, rows:]
-    groups = lax.axis_size("dp")
-    packed = pack_totals(totals, groups)
-    wide = lax.psum_scatter(packed, "dp", scatter_dimension=0, tiled=True)
-    summed_row = lax.psum(wide.astype(jnp.bfloat16), "section").astype(jnp.float32)[0]
-    summed = unpack_totals(summed_row, totals, groups)
-    return (finals_shard, frames_shard) + tuple(summed)
+    outputs, frame_grads = [], []
+    layer_terms = [None, None]
+    table_terms, final_terms = None, None
+
+    def plus(total, terms):
+        return terms if total is None else tuple(a + b for a, b in zip(total, terms))
+
+    for part in range(per):
+        slot = section * per + part
+        position, allowed = token_layout(kinds[slot], steps, slots)
+        hidden = embed_forward(tables, frames[slot], actions[slot], deltas[slot], position)
+        caches = []
+        for depth in range(2):
+            hidden, cache = layer_forward(hidden, layer_weights(depth), allowed)
+            caches.append(cache)
+        output, pull = jax.vjp(norm_apply, hidden.astype(jnp.float32), final_gain, final_bias)
+        grad_hidden, grad_gain, grad_bias = pull(cotangent[slot].astype(jnp.float32))
+        final_terms = plus(final_terms, (grad_gain, grad_bias))
+        grad = grad_hidden.astype(jnp.bfloat16)
+        for depth in (1, 0):
+            grad, terms = layer_backward(caches[depth], layer_weights(depth), allowed, grad)
+            layer_terms[depth] = plus(layer_terms[depth], terms)
+        frame_grad, terms = embed_backward(tables, actions[slot], deltas[slot], position, grad)
+        table_terms = plus(table_terms, terms)
+        outputs.append(output)
+        frame_grads.append(frame_grad)
+
+    big = {}
+    for depth in (1, 0):
+        terms = layer_terms[depth]
+        big[depth] = [reduced(terms[k]) for k in (9, 2, 5)] + [reduced(terms[11].T)]
+    codes = [reduced(t.T) for t in table_terms]
+    small = [
+        jnp.stack([layer_terms[0][k], layer_terms[1][k]], axis=1).reshape(width, -1) if k != 10
+        else jnp.concatenate([layer_terms[d][k].reshape(width, -1) for d in (0, 1)], axis=1)
+        for k in (0, 1, 3, 4, 6, 7, 8, 10, 12)
+    ] + [t[:, None] for t in final_terms]
+    widths = [s.shape[1] for s in small]
+    joined = reduced(jnp.concatenate(small, axis=1))
+    pieces = []
+    start = 0
+    for w in widths:
+        pieces.append(joined[:, start : start + w])
+        start += w
+
+    def vec(piece):
+        half = piece.shape[1] // 2
+        return jnp.stack([piece[:, :half].reshape(-1), piece[:, half:].reshape(-1)])
+
+    gain1, bias1, qb, vb, outb, gain2, bias2, upb, downb, fg, fb = pieces
+    both = [jnp.stack([big[0][k], big[1][k]]) for k in range(4)]
+    return (
+        jnp.stack(outputs),
+        jnp.stack(frame_grads),
+        codes[0].T,
+        codes[1].T,
+        codes[2].T,
+        vec(gain1),
+        vec(bias1),
+        both[1],
+        vec(qb),
+        vec(vb),
+        both[2],
+        vec(outb),
+        vec(gain2),
+        vec(bias2),
+        both[0],
+        vec(upb),
+        both[3].transpose(0, 2, 1),
+        vec(downb),
+        fg[:, 0],
+        fb[:, 0],
+    )
 
 
 def solution(mesh):

time: 4260 us -> 1980 us (0.46)
  blocking collectives: 1060 us -> 68.3 us
  local copies, waits for them, and re-layouts: 610 us -> 73 us
  starting transfers between devices: 479 us -> 0.71 us
  waiting for transfers between devices: 1640 us -> 1390 us
  matrix products: 90.5 us -> 321 us
  loops' own time: 157 us -> 0 us
  other arithmetic: 199 us -> 93.7 us
    ppermute x14 -> x0, waiting for transfers between devices: 1570 us -> none  [passed_along(): return lax.ppermute(array, axis, pairs)]
    reduce_scatter x1 -> x12, waiting for transfers between devices: 0.01 us -> 1390 us  [reduced(): lax.psum_scatter(matrix.astype(jnp.bfloat16), ('dp', 'section'), scatter_...]
    unnamed x1 -> x0, blocking collectives: 1060 us -> none
    ppermute x14 -> x0, starting transfers between devices: 479 us -> none  [passed_along(): return lax.ppermute(array, axis, pairs)]
    dot_general x0 -> x18, matrix products: none -> 171 us  [the longest x2 42.9 us: layer_backward(): jnp.einsum('qhd,khd->hqk', grad_mixed_bits, value_part, preferred_element...]
    dynamic_slice x91 -> x4, local copies, waits for them, and re-layouts: 170 us -> 2.81 us  [the longest x1 1.32 us: local(): position, allowed = token_layout(kinds[slot], steps, slots)]
    dynamic_update_slice x42 -> x0, other arithmetic: 164 us -> none  [the longest x28 137 us: forward_tick(): lax.dynamic_update_index_in_dim(store, jnp.where(valid, piece, store[slot...]
    another operation x16 -> x0, loops' own time: 157 us -> none  [the longest x7 119 us: forward_tick(): lax.switch(section, [forward_first_section, layer_section(0), layer_secti...]
  transfers between devices with their start and end apart: 16 -> 12, of which waited for: 8 -> 12; matrix products, arithmetic and copies ran while one was open for 9% -> 4% of each run, Pallas kernels for 0% -> 0%
where the time goes in v1:
time: 1980 us; the launch traced here: 1970 us
  waiting for transfers between devices  1390 us (70%)
  matrix products  321 us (16%)
  other arithmetic  93.7 us (5%)
  local copies, waits for them, and re-layouts  73 us (4%)
  blocking collectives  68.3 us (3%)
    reduce_scatter x12, waiting for transfers between devices, reduced(): lax.psum_scatter(matrix.astype(jnp.bfloat16), ('dp', 'section'), scatter_...  1390 us
    all_gather x12, blocking collectives, reduced(): lax.all_gather(shard, 'section', axis=0, tiled=True).astype(jnp.float32)  68.3 us
    dot_general x11, matrix products, plain_product(): return jnp.dot(left, right, preferred_element_type=jnp.float32)  57.9 us
    convert_element_type x2, other arithmetic, layer_backward(): grad_scores = (probs * (grad_probs - inner)).astype(jnp.bfloat16)  55.8 us
    dot_general x11, matrix products, left_product(): lax.dot_general(left, right, (((0,), (0,)), ((), ())), preferred_element_...  48.7 us
    sub x2, matrix products, attention_probs(): shifted = jnp.exp(scores - jnp.max(scores, axis=-1, keepdims=True))  43.1 us
    dot_general x2, matrix products, layer_backward(): jnp.einsum('qhd,khd->hqk', grad_mixed_bits, value_part, preferred_element...  42.9 us
  transfers between devices with their start and end apart: 12, of which 12 were waited for; matrix products, arithmetic and copies ran while one was open for 4% of the time, Pallas kernels for 0%

profile of v1, /device:TPU:0, one launch (start us, length us, event | category | flops | bytes accessed | tf_op | source)
XLA Modules:
  0.0 1966.6 jit_solution(9932903583376237305)
XLA Ops:
  46.7 16.1 fusion.186
  62.9 12.4 fusion.97
  78.6 22.2 %multiply_convert_fusion.3 = (bf16[1008,2048]{1,0:T(8,128)(2,1)S(1)}, f32[1008,2048]{1,0:T(8,128)}, f32[1008,2048]{1,0:T(8,128)}) fusion(f32[2048]{0:T(1024)S(1)} %bitcast.288, bf16[2,512,2048]{2,1,0:T(8,128)(2,1)S(1)} %copy-done.103, f32[1008,512]{1,0:T(8,128)S(1)} %get-tuple-element.214, f32[512]{0:T(512)S(1)} %bitcast.274, f32[512]{0:T(512)S(1)} %bitcast.266, ...), kind=kOutput, calls=%fused_computation.43 | convolution fusion | flops 2252759040 | bytes 24825856 | tf_op jit(solution)/shard_map/dot_general | solution.py:35
  112.8 26.9 %fusion.188 = (f32[8,1008]{1,0:T(8,128)S(1)}, f32[8,1008,1008]{1,2,0:T(8,128)}) fusion(pred[1008,1008]{0,1:T(8,128)(4,1)} %compare_and_fusion, bf16[1008,8,64]{0,2,1:T(8,128)(2,1)S(1)} %bitcast.242, bf16[1008,8,64]{0,2,1:T(8,128)(2,1)S(1)} %bitcast.240), kind=kOutput, calls=%fused_computation.321 | convolution fusion | flops 1072964608 | bytes 35626752 | tf_op jit(solution)/shard_map/sub | solution.py:115
  139.8 12.4 fusion.103
  155.6 22.0 %multiply_convert_fusion.2 = (bf16[1008,2048]{1,0:T(8,128)(2,1)S(1)}, f32[1008,2048]{1,0:T(8,128)}, f32[1008,2048]{1,0:T(8,128)}) fusion(f32[2048]{0:T(1024)S(1)} %bitcast.290, bf16[2,512,2048]{2,1,0:T(8,128)(2,1)S(1)} %copy-done.104, f32[1008,512]{1,0:T(8,128)S(1)} %get-tuple-element.221, f32[512]{0:T(512)S(1)} %bitcast.276, f32[512]{0:T(512)S(1)} %bitcast.270, ...), kind=kOutput, calls=%fused_computation.26 | convolution fusion | flops 2252759040 | bytes 24825856 | tf_op jit(solution)/shard_map/dot_general | solution.py:35
  205.5 14.5 fusion.106
  219.9 21.4 %multiply_reduce_fusion.1 = (f32[8,1008]{1,0:T(8,128)S(1)}, f32[8,1008,1008]{1,2,0:T(8,128)}) fusion(f32[8,1008,1008]{1,2,0:T(8,128)} %get-tuple-element.219, f32[8,1008]{1,0:T(8,128)S(1)} %get-tuple-element.218, bf16[1008,8,64]{0,2,1:T(8,128)(2,1)} %bitcast.255, bf16[1008,8,64]{0,2,1:T(8,128)(2,1)S(1)} %bitcast.253), kind=kOutput, calls=%fused_computation.5 | convolution fusion | flops 1064827008 | bytes 67156992 | tf_op jit(solution)/shard_map/qhd,khd->hqk/dot_general | solution.py:195
  241.4 27.7 %multiply_convert_fusion.1 = bf16[8,1008,1008]{1,2,0:T(8,128)(2,1)} fusion(f32[8,1008,1008]{1,2,0:T(8,128)} %get-tuple-element.227, f32[8,1008]{1,0:T(8,128)S(1)} %get-tuple-element.226, f32[8,1008,1008]{1,2,0:T(8,128)} %get-tuple-element.219, f32[8,1008]{1,0:T(8,128)S(1)} %get-tuple-element.218), kind=kLoop, calls=%fused_computation.4 | loop fusion | flops 32514048 | bytes 81349632 | tf_op jit(solution)/shard_map/convert_element_type | solution.py:205
  314.6 14.5 fusion.100
  329.1 21.4 %multiply_reduce_fusion = (f32[8,1008]{1,0:T(8,128)S(1)}, f32[8,1008,1008]{1,2,0:T(8,128)}) fusion(f32[8,1008,1008]{1,2,0:T(8,128)} %get-tuple-element.212, f32[8,1008]{1,0:T(8,128)S(1)} %copy-done.70, bf16[1008,8,64]{0,2,1:T(8,128)(2,1)} %bitcast.257, bf16[1008,8,64]{0,2,1:T(8,128)(2,1)S(1)} %bitcast.251), kind=kOutput, calls=%fused_computation.3 | convolution fusion | flops 1064827008 | bytes 67156992 | tf_op jit(solution)/shard_map/qhd,khd->hqk/dot_general | solution.py:195
  350.6 28.0 %multiply_convert_fusion = bf16[8,1008,1008]{1,2,0:T(8,128)(2,1)} fusion(f32[8,1008,1008]{1,2,0:T(8,128)} %get-tuple-element.231, f32[8,1008]{1,0:T(8,128)S(1)} %get-tuple-element.230, f32[8,1008,1008]{1,2,0:T(8,128)} %get-tuple-element.212, f32[8,1008]{1,0:T(8,128)S(1)} %copy-done.70), kind=kLoop, calls=%fused_computation.2 | loop fusion | flops 32514048 | bytes 81349632 | tf_op jit(solution)/shard_map/convert_element_type | solution.py:205
  487.9 60.9 %reduce-scatter.17.cloned.1.call-done = bf16[16,17]{1,0:T(8,128)(2,1)} async-done(((bf16[512,17]{1,0:T(8,128)(2,1)}), bf16[16,17]{1,0:T(8,128)(2,1)}) %reduce-scatter.17.cloned.1.call-update) | async-done | bytes 560 | tf_op jit(solution)/shard_map/reduce_scatter | solution.py:247
  554.9 126.0 %reduce-scatter.37.cloned.1.call-done = bf16[16,26]{1,0:T(8,128)(2,1)} async-done(((bf16[512,26]{1,0:T(8,128)(2,1)}), bf16[16,26]{1,0:T(8,128)(2,1)}) %reduce-scatter.37.cloned.1.call-update) | async-done | bytes 848 | tf_op jit(solution)/shard_map/reduce_scatter | solution.py:247
  690.5 123.0 %reduce-scatter.19.cloned.1.call-done = bf16[16,126]{1,0:T(8,128)(2,1)} async-done(((bf16[512,126]{1,0:T(8,128)(2,1)}), bf16[16,126]{1,0:T(8,128)(2,1)}) %reduce-scatter.19.cloned.1.call-update) | async-done | bytes 4048 | tf_op jit(solution)/shard_map/reduce_scatter | solution.py:247
  819.4 126.1 %reduce-scatter.27.cloned.1.call-done = bf16[16,512]{1,0:T(8,128)(2,1)} async-done(((bf16[512,512]{1,0:T(8,128)(2,1)}), bf16[16,512]{1,0:T(8,128)(2,1)}) %reduce-scatter.27.cloned.1.call-update) | async-done | bytes 16400 | tf_op jit(solution)/shard_map/reduce_scatter | solution.py:247
  951.0 126.2 %reduce-scatter.25.cloned.1.call-done = bf16[16,512]{1,0:T(8,128)(2,1)} async-done(((bf16[512,512]{1,0:T(8,128)(2,1)}), bf16[16,512]{1,0:T(8,128)(2,1)}) %reduce-scatter.25.cloned.1.call-update) | async-done | bytes 16400 | tf_op jit(solution)/shard_map/reduce_scatter | solution.py:247
  1083.4 126.8 %reduce-scatter.15.cloned.1.call-done = bf16[16,1024]{1,0:T(8,128)(2,1)} async-done(((bf16[512,1024]{1,0:T(8,128)(2,1)}), bf16[16,1024]{1,0:T(8,128)(2,1)}) %reduce-scatter.15.cloned.1.call-update) | async-done | bytes 32784 | tf_op jit(solution)/shard_map/reduce_scatter | solution.py:247
  1215.8 92.6 %reduce-scatter.23.cloned.1.call-done = bf16[16,1536]{1,0:T(8,128)(2,1)} async-done(((bf16[512,1536]{1,0:T(8,128)(2,1)}), bf16[16,1536]{1,0:T(8,128)(2,1)}) %reduce-scatter.23.cloned.1.call-update) | async-done | bytes 49168 | tf_op jit(solution)/shard_map/reduce_scatter | solution.py:247
  1314.3 95.4 %reduce-scatter.21.cloned.1.call-done = bf16[16,1536]{1,0:T(8,128)(2,1)} async-done(((bf16[512,1536]{1,0:T(8,128)(2,1)}), bf16[16,1536]{1,0:T(8,128)(2,1)}) %reduce-scatter.21.cloned.1.call-update) | async-done | bytes 49168 | tf_op jit(solution)/shard_map/reduce_scatter | solution.py:247
  1417.2 130.6 %reduce-scatter.35.cloned.1.call-done = bf16[16,2048]{1,0:T(8,128)(2,1)} async-done(((bf16[512,2048]{1,0:T(8,128)(2,1)}), bf16[16,2048]{1,0:T(8,128)(2,1)}) %reduce-scatter.35.cloned.1.call-update) | async-done | bytes 65552 | tf_op jit(solution)/shard_map/reduce_scatter | solution.py:247
  1553.8 128.9 %reduce-scatter.31.cloned.1.call-done = bf16[16,2048]{1,0:T(8,128)(2,1)} async-done(((bf16[512,2048]{1,0:T(8,128)(2,1)}), bf16[16,2048]{1,0:T(8,128)(2,1)}) %reduce-scatter.31.cloned.1.call-update) | async-done | bytes 65552 | tf_op jit(solution)/shard_map/reduce_scatter | solution.py:247
  1688.7 128.9 %reduce-scatter.33.cloned.1.call-done = bf16[16,2048]{1,0:T(8,128)(2,1)} async-done(((bf16[512,2048]{1,0:T(8,128)(2,1)}), bf16[16,2048]{1,0:T(8,128)(2,1)}) %reduce-scatter.33.cloned.1.call-update) | async-done | bytes 65552 | tf_op jit(solution)/shard_map/reduce_scatter | solution.py:247
  1824.6 127.8 %reduce-scatter.29.cloned.1.call-done = bf16[16,2048]{1,0:T(8,128)(2,1)} async-done(((bf16[512,2048]{1,0:T(8,128)(2,1)}), bf16[16,2048]{1,0:T(8,128)(2,1)}) %reduce-scatter.29.cloned.1.call-update) | async-done | bytes 65552 | tf_op jit(solution)/shard_map/reduce_scatter | solution.py:247
  (432 shorter events, 316.8 us)
Async XLA Ops:
  7.2 541.6 %reduce-scatter.17.cloned.1.call-start = ((), (), s32[]{:S(2)}) async-start(), calls=%async_computation.13 | async-start | bytes 135168 | tf_op jit(solution)/shard_map/reduce_scatter | solution.py:247
  17.7 59.0 %copy-start.47 = (f32[1,512]{1,0:T(1,128)}, f32[1,512]{1,0:T(1,128)S(1)}, u32[]{:S(2)}) copy-start(f32[1,512]{1,0:T(1,128)S(1)} %get-tuple-element.194) | copy-start | bytes 6148
  19.0 57.6 %copy-start.55 = (f32[1,512]{1,0:T(1,128)}, f32[1,512]{1,0:T(1,128)S(1)}, u32[]{:S(2)}) copy-start(f32[1,512]{1,0:T(1,128)S(1)} %get-tuple-element.196) | copy-start | bytes 6148
  21.8 54.9 %copy-start.79 = (f32[1,2048]{1,0:T(1,128)}, f32[1,2048]{1,0:T(1,128)S(1)}, u32[]{:S(2)}) copy-start(f32[1,2048]{1,0:T(1,128)S(1)} %get-tuple-element.184) | copy-start | bytes 24580
  36.5 38.8 %copy-start.7 = (bf16[1008,512]{1,0:T(8,128)(2,1)}, bf16[1008,512]{1,0:T(8,128)(2,1)S(1)}, u32[]{:S(2)}) copy-start(bf16[1008,512]{1,0:T(8,128)(2,1)S(1)} %get-tuple-element.210) | copy-start | bytes 3096580
  103.3 48.9 %copy-start.9 = (bf16[1008,512]{1,0:T(8,128)(2,1)}, bf16[1008,512]{1,0:T(8,128)(2,1)S(1)}, u32[]{:S(2)}) copy-start(bf16[1008,512]{1,0:T(8,128)(2,1)S(1)} %get-tuple-element.217) | copy-start | bytes 3096580
  108.3 31.5 %copy-start.25 = (bf16[1008,512]{0,1:T(8,128)(2,1)}, bf16[1008,512]{0,1:T(8,128)(2,1)S(1)}, u32[]{:S(2)}) copy-start(bf16[1008,512]{0,1:T(8,128)(2,1)S(1)} %copy.167) | copy-start | bytes 3096580
  110.2 29.6 %copy-start.26 = (bf16[1008,512]{0,1:T(8,128)(2,1)}, bf16[1008,512]{0,1:T(8,128)(2,1)S(1)}, u32[]{:S(2)}) copy-start(bf16[1008,512]{0,1:T(8,128)(2,1)S(1)} %copy.166) | copy-start | bytes 3096580
  153.1 46.6 %copy-start.4 = (f32[1008,512]{1,0:T(8,128)}, f32[1008,512]{1,0:T(8,128)S(1)}, u32[]{:S(2)}) copy-start(f32[1008,512]{1,0:T(8,128)S(1)} %get-tuple-element.221) | copy-start | bytes 6193156
  153.1 46.6 %copy-start.40 = (f32[1008]{0:T(1024)}, f32[1008]{0:T(1024)S(1)}, u32[]{:S(2)}) copy-start(f32[1008]{0:T(1024)S(1)} %broadcast_multiply_fusion.1) | copy-start | bytes 12100
  153.6 46.1 %copy-start.44 = (f32[1008]{0:T(1024)}, f32[1008]{0:T(1024)S(1)}, u32[]{:S(2)}) copy-start(f32[1008]{0:T(1024)S(1)} %fusion.144) | copy-start | bytes 12100
  350.5 28.0 %copy-start.24 = (bf16[1008,512]{0,1:T(8,128)(2,1)S(1)}, bf16[1008,512]{0,1:T(8,128)(2,1)}, u32[]{:S(2)}) copy-start(bf16[1008,512]{0,1:T(8,128)(2,1)} %copy-done.23) | copy-start | bytes 3096580
  412.2 268.7 %reduce-scatter.37.cloned.1.call-start = ((), (), s32[]{:S(2)}) async-start(), calls=%async_computation.23 | async-start | bytes 135168 | tf_op jit(solution)/shard_map/reduce_scatter | solution.py:247
  433.6 379.9 %reduce-scatter.19.cloned.1.call-start = ((), (), s32[]{:S(2)}) async-start(), calls=%async_computation.14 | async-start | bytes 135168 | tf_op jit(solution)/shard_map/reduce_scatter | solution.py:247
  436.2 509.4 %reduce-scatter.27.cloned.1.call-start = ((), (), s32[]{:S(2)}) async-start(), calls=%async_computation.18 | async-start | bytes 540672 | tf_op jit(solution)/shard_map/reduce_scatter | solution.py:247
  439.3 637.9 %reduce-scatter.25.cloned.1.call-start = ((), (), s32[]{:S(2)}) async-start(), calls=%async_computation.17 | async-start | bytes 540672 | tf_op jit(solution)/shard_map/reduce_scatter | solution.py:247
  442.5 767.7 %reduce-scatter.15.cloned.1.call-start = ((), (), s32[]{:S(2)}) async-start(), calls=%async_computation.12 | async-start | bytes 1081344 | tf_op jit(solution)/shard_map/reduce_scatter | solution.py:247
  450.5 857.8 %reduce-scatter.23.cloned.1.call-start = ((), (), s32[]{:S(2)}) async-start(), calls=%async_computation.16 | async-start | bytes 1622016 | tf_op jit(solution)/shard_map/reduce_scatter | solution.py:247
  456.2 953.5 %reduce-scatter.21.cloned.1.call-start = ((), (), s32[]{:S(2)}) async-start(), calls=%async_computation.15 | async-start | bytes 1622016 | tf_op jit(solution)/shard_map/reduce_scatter | solution.py:247
  461.6 1086.2 %reduce-scatter.35.cloned.1.call-start = ((), (), s32[]{:S(2)}) async-start(), calls=%async_computation.22 | async-start | bytes 2162688 | tf_op jit(solution)/shard_map/reduce_scatter | solution.py:247
  467.9 1214.7 %reduce-scatter.31.cloned.1.call-start = ((), (), s32[]{:S(2)}) async-start(), calls=%async_computation.20 | async-start | bytes 2162688 | tf_op jit(solution)/shard_map/reduce_scatter | solution.py:247
  475.0 1342.5 %reduce-scatter.33.cloned.1.call-start = ((), (), s32[]{:S(2)}) async-start(), calls=%async_computation.21 | async-start | bytes 2162688 | tf_op jit(solution)/shard_map/reduce_scatter | solution.py:247
  481.0 1471.4 %reduce-scatter.29.cloned.1.call-start = ((), (), s32[]{:S(2)}) async-start(), calls=%async_computation.19 | async-start | bytes 2162688 | tf_op jit(solution)/shard_map/reduce_scatter | solution.py:247
  1308.4 651.0 %copy-start.1 = (bf16[1024,512]{1,0:T(8,128)(2,1)S(1)}, bf16[1024,512]{1,0:T(8,128)(2,1)}, u32[]{:S(2)}) copy-start(bf16[1024,512]{1,0:T(8,128)(2,1)} %param.27) | copy-start | bytes 3145732
  (107 other events, 874.0 us)
Sparse Core Ops, SparseCore 0:
  412.3 136.4 reduce-scatter.16
  551.1 129.7 reduce-scatter.36
  683.7 129.6 reduce-scatter.18
  815.6 129.8 reduce-scatter.26
  947.6 129.5 reduce-scatter.24
  1079.4 130.6 reduce-scatter.14
  1215.4 92.9 reduce-scatter.22
  1313.6 96.0 reduce-scatter.20
  1412.0 135.7 reduce-scatter.34
  1550.0 132.5 reduce-scatter.30
  1684.9 132.5 reduce-scatter.32
  1819.8 132.5 reduce-scatter.28
